TPU v7x, 256 devices: a whole 4x4x8 slice. The times are simulated.
256 devices in a mesh: dp: 16 (over x_lo, z), ctx: 16 (over y, x_hi, core).
Axes of the slice: x: 4 (x_hi: 2, x_lo: 2; x = x_hi * 2 + x_lo), y: 4, z: 8, core: 2. Of those that a mesh axis runs over, the one named last changes fastest.
Arguments:
- hidden: bfloat16 [16, 2048, 4096], P('dp', 'ctx'), may hold values from -6 to 6
- value_weight: bfloat16 [4096, 512], P(('dp', 'ctx')), may hold values from -0.09375 to 0.09375
- queries: bfloat16 [16, 2048, 4096], P('dp', 'ctx'), may hold values from -4.5 to 4.5
- key_rows: bfloat16 [16, 2048, 512], P('dp', 'ctx'), may hold values from -4.5 to 4.5
- attn_saved: bfloat16 [16, 2048, 4096], P('dp', 'ctx'), may hold values from -3 to 3
- grad_out: bfloat16 [16, 2048, 4096], P('dp', 'ctx'), may hold values from -6 to 6
- doc_lengths: int32 [16, 8], P('dp'), may hold values from 1 to 1024, 2048 in all within a row
- routing: int32 [16, 2048], P('dp'), may hold values from 0 to 2047, as said below
- visible_blocks: int32 [16, 32, 32], P('dp'), may hold values from 0 to 1, as said below
Outputs:
- grad_query: bfloat16 [16, 2048, 4096], P('dp', 'ctx')
- grad_key: bfloat16 [16, 2048, 512], P('dp', 'ctx')
- grad_value_weight: float32 [4096, 512], P(('dp', 'ctx'))
Inputs may be any that keep to these rules, and one draw needn't show every extreme that they name: For each pack, routing is a permutation: the token at position i, held by device i // 128 of ctx, goes to owner slot routing[i], held by device routing[i] // 128 of ctx, so every owner device receives 128 tokens. At most 16 tokens of one device go to one owner device, and this bound is reached in every draw. visible_blocks[b, b] = 1 for every block b. `doc_lengths`: each pack's lengths sum to 2048; the longest is 1024.
All inputs are finite; a program needn't handle non-finite values.
Results may differ from a plain program's by a relative error of at most 0.023.
Values may be sent and summed in bfloat16 or wider, within the bound.
A program may use at most 128 MiB of HBM per device.

v0:
```python
import math
import jax
import jax.numpy as jnp
from jax import lax
from jax.sharding import PartitionSpec as P

QH = 32
KVH = 4
HD = 128
VB = 64
far_below = -1e30


def document_index(positions, doc_lengths):
    doc_ends = jnp.cumsum(doc_lengths)
    return jnp.sum((positions[:, None] >= doc_ends[None, :]).astype(jnp.int32), axis=1)


def merge_pairs(first, second):
    top = jnp.maximum(first[0], second[0])
    return (top, first[1] * jnp.exp(first[0] - top) + second[1] * jnp.exp(second[0] - top))


def local(
    hidden,
    value_weight,
    queries,
    key_rows,
    attn_saved,
    grad_out,
    doc_lengths,
    routing,
    visible_blocks,
):
    row_count = hidden.shape[1]
    ctx_count = lax.axis_size("ctx")
    dp_count = lax.axis_size("dp")
    ctx_place = lax.axis_index("ctx")
    token_count = routing.shape[1]
    capacity = 2 * row_count // ctx_count
    slot_count = ctx_count * capacity
    group_size = QH // KVH
    kv_width = key_rows.shape[2]
    score_scale = 1.0 / math.sqrt(HD)
    features = hidden[0]
    slot_route = routing[0]
    lengths = doc_lengths[0]
    block_table = visible_blocks[0].astype(jnp.float32)
    block_count = block_table.shape[0]
    columns = features
    projected = jnp.dot(
        columns,
        lax.all_gather(value_weight, ("dp", "ctx"), axis=0, tiled=True),
        preferred_element_type=jnp.float32,
    )
    value_rows = projected.astype(jnp.bfloat16)
    token_iota = jnp.arange(token_count, dtype=jnp.int32)
    slot_position = jnp.zeros((token_count,), jnp.int32).at[slot_route].set(token_iota)
    query_position = lax.dynamic_slice_in_dim(slot_position, ctx_place * row_count, row_count)
    local_route = lax.dynamic_slice_in_dim(slot_route, ctx_place * row_count, row_count)
    device_iota = jnp.arange(ctx_count, dtype=jnp.int32)
    target = local_route // row_count
    matches = (target[:, None] == device_iota[None, :]).astype(jnp.int32)
    earlier = jnp.cumsum(matches, axis=0) - matches
    send_slot = target * capacity + jnp.sum(earlier * matches, axis=1)
    buffer_iota = jnp.arange(slot_count, dtype=jnp.int32)
    send_matrix = (buffer_iota[:, None] == send_slot[None, :]).astype(jnp.bfloat16)
    owner_table = slot_route.reshape(ctx_count, row_count) // row_count
    coming = (owner_table == ctx_place).astype(jnp.int32)
    arrival = (device_iota[:, None] * capacity + jnp.cumsum(coming, axis=1) - coming).reshape(
        token_count
    )
    arrive_slot = arrival[query_position]
    receive_matrix = (arrive_slot[:, None] == buffer_iota[None, :]).astype(jnp.bfloat16)

    def to_slots(source_rows):
        placed = jnp.dot(send_matrix, source_rows, preferred_element_type=jnp.float32).astype(
            jnp.bfloat16
        )
        return placed.reshape(ctx_count, capacity, source_rows.shape[1])

    def from_slots(arrived):
        flat_rows = arrived.reshape(slot_count, arrived.shape[2])
        return jnp.dot(receive_matrix, flat_rows, preferred_element_type=jnp.float32).astype(
            jnp.bfloat16
        )

    local_pair = jnp.concatenate([key_rows[0], value_rows], axis=1)
    got_query, got_grad, got_pair = (
        lax.all_to_all(to_slots(queries[0]), "ctx", split_axis=0, concat_axis=0, tiled=True),
        lax.all_to_all(to_slots(grad_out[0]), "ctx", split_axis=0, concat_axis=0, tiled=True),
        lax.all_to_all(to_slots(local_pair), "ctx", split_axis=0, concat_axis=0, tiled=True),
    )
    pair_rows = from_slots(got_pair)
    owner_query = from_slots(got_query)
    owner_grad = from_slots(got_grad)
    pair_whole = lax.all_gather(pair_rows, "ctx", axis=0, tiled=True)
    query_docs = document_index(query_position, lengths)
    key_docs = document_index(slot_position, lengths)
    block_iota = jnp.arange(block_count, dtype=jnp.int32)
    query_onehot = (query_position[:, None] // VB == block_iota[None, :]).astype(jnp.float32)
    row_visible = jnp.dot(query_onehot, block_table, preferred_element_type=jnp.float32)
    key_onehot = (slot_position[:, None] // VB == block_iota[None, :]).astype(jnp.float32)
    visible = jnp.dot(row_visible, key_onehot.T, preferred_element_type=jnp.float32)
    allowed = (
        (query_docs[:, None] == key_docs[None, :])
        & (slot_position[None, :] <= query_position[:, None])
        & (visible > 0.5)
    )
    presence = jnp.broadcast_to(
        allowed.astype(jnp.float32)[None], (group_size, row_count, token_count)
    )
    query_heads = owner_query.reshape(row_count, KVH, group_size, HD)
    grad_heads = owner_grad.reshape(row_count, KVH, group_size, HD)
    saved_heads = attn_saved[0].astype(jnp.float32).reshape(row_count, KVH, group_size, HD)
    row_delta = jnp.transpose(
        jnp.sum(grad_heads.astype(jnp.float32) * saved_heads, axis=-1), (1, 2, 0)
    )
    key_all = pair_whole[:, :kv_width].reshape(token_count, KVH, HD)
    value_all = pair_whole[:, kv_width:].reshape(token_count, KVH, HD)
    query_parts = []
    key_parts = []
    value_parts = []
    for kv_head in range(KVH):
        head_query = query_heads[:, kv_head]
        head_grad = grad_heads[:, kv_head]
        head_keys = key_all[:, kv_head]
        scores = (
            jnp.einsum("rjd,kd->jrk", head_query, head_keys, preferred_element_type=jnp.float32)
            * score_scale
        )
        masked = jnp.where(allowed[None], scores, far_below)
        row_top, row_total = lax.reduce(
            (masked, presence), (jnp.float32(far_below), jnp.float32(0.0)), merge_pairs, (2,)
        )
        log_total = (row_top + jnp.log(row_total))[..., None]
        weights = jnp.where(allowed[None], jnp.exp(scores - log_total), 0.0)
        weights_b = weights.astype(jnp.bfloat16)
        dweights = jnp.einsum(
            "rjd,kd->jrk", head_grad, value_all[:, kv_head], preferred_element_type=jnp.float32
        ).astype(jnp.bfloat16)
        dscores = (
            score_scale * weights * (dweights.astype(jnp.float32) - row_delta[kv_head][..., None])
        ).astype(jnp.bfloat16)
        query_parts.append(
            jnp.einsum("jrk,kd->rjd", dscores, head_keys, preferred_element_type=jnp.float32)
        )
        key_parts.append(
            jnp.einsum("jrk,rjd->kd", dscores, head_query, preferred_element_type=jnp.float32)
        )
        value_parts.append(
            jnp.einsum("jrk,rjd->kd", weights_b, head_grad, preferred_element_type=jnp.float32)
        )
    query_grad = jnp.stack(query_parts, axis=1)
    pair_terms = jnp.concatenate(
        [jnp.concatenate(key_parts, axis=1), jnp.concatenate(value_parts, axis=1)], axis=1
    )
    pair_sums = lax.psum_scatter(
        pair_terms.astype(jnp.bfloat16), "ctx", scatter_dimension=0, tiled=True
    )
    outgoing = jnp.dot(receive_matrix.T, pair_sums, preferred_element_type=jnp.float32).astype(
        jnp.bfloat16
    )
    returned = lax.all_to_all(
        outgoing.reshape(ctx_count, capacity, 2 * kv_width),
        "ctx",
        split_axis=0,
        concat_axis=0,
        tiled=True,
    )
    loader_grad = jnp.dot(
        send_matrix.T,
        returned.reshape(slot_count, 2 * kv_width),
        preferred_element_type=jnp.float32,
    ).astype(jnp.bfloat16)
    grad_value = loader_grad[:, kv_width:]
    weight_scale = 1.0 / math.sqrt(dp_count * token_count)
    columns = features
    weight_grad = lax.psum_scatter(
        jnp.einsum("rd,rk->dk", columns, grad_value, preferred_element_type=jnp.float32)
        * weight_scale,
        ("dp", "ctx"),
        scatter_dimension=0,
        tiled=True,
    )
    grad_query = query_grad.reshape(row_count, QH * HD).astype(jnp.bfloat16)
    return (grad_query[None], loader_grad[:, :kv_width][None], weight_grad)


def solution(mesh):
    placed = (
        P("dp", "ctx", None),
        P(("dp", "ctx"), None),
        P("dp", "ctx", None),
        P("dp", "ctx", None),
        P("dp", "ctx", None),
        P("dp", "ctx", None),
        P("dp", None),
        P("dp", None),
        P("dp", None, None),
    )
    return jax.shard_map(
        local,
        mesh=mesh,
        in_specs=placed,
        out_specs=(P("dp", "ctx", None), P("dp", "ctx", None), P(("dp", "ctx"), None)),
        check_vma=False,
    )
```

profile of v0, /device:TPU:128, one launch (start us, length us, event | category | flops | bytes accessed | tf_op | source)
XLA Modules:
  0.0 2082.8 jit_solution(7185739076317425619)
XLA Ops:
  8.6 8.0 scatter_custom_fusion
  19.3 405.7 %all-gather.3.cloned.1.call-done = bf16[4096,512]{1,0:T(8,128)(2,1)} async-done(((bf16[16,512]{1,0:T(8,128)(2,1)}), bf16[4096,512]{1,0:T(8,128)(2,1)}) %all-gather.3.cloned.1.call-update) | async-done | bytes 4194320 | tf_op jit(solution)/shard_map/all_gather | solution.py:53
  429.9 3.6 all-to-all-start
  435.8 10.0 all-to-all-done
  448.8 3.7 all-to-all-start.2
  452.6 3.3 convolution_convert_fusion.1
  455.8 28.8 %all-to-all-done.2 = bf16[16,16,4096]{2,1,0:T(8,128)(2,1)S(1)} async-done(((bf16[16,16,4096]{2,1,0:T(8,128)(2,1)}), bf16[16,16,4096]{2,1,0:T(8,128)(2,1)S(1)}, u32[]{:S(2)}, u32[]{:S(2)}) %all-to-all-start.2) | async-done | bytes 2097184 | tf_op jit(solution)/shard_map/all_to_all | solution.py:91
  484.6 4.4 all-to-all-start.1
  498.5 31.1 %all-to-all-done.1 = bf16[16,16,4096]{2,1,0:T(8,128)(2,1)} async-done(((bf16[16,16,4096]{2,1,0:T(8,128)(2,1)}), bf16[16,16,4096]{2,1,0:T(8,128)(2,1)}, u32[]{:S(2)}, u32[]{:S(2)}) %all-to-all-start.1) | async-done | bytes 2097184 | tf_op jit(solution)/shard_map/all_to_all | solution.py:90
  541.9 4.6 fusion.140
  546.5 4.1 reshape.213
  550.6 4.0 reshape.207
  554.6 8.9 fusion.142
  563.5 4.3 fusion.141
  569.1 3.4 fusion.17
  572.5 3.4 fusion.16
  579.6 3.4 fusion.7
  585.4 4.5 fusion.12
  592.5 4.7 fusion.2
  597.2 6.7 fusion.11
  606.3 6.2 fusion.6
  612.5 4.5 fusion.53
  617.0 4.3 fusion.1
  625.6 3.8 fusion.68
  637.4 6.4 copy.240
  643.9 85.8 %reduce-scatter.7.cloned.1.call-done = bf16[128,1024]{1,0:T(8,128)(2,1)} async-done(((bf16[2048,1024]{1,0:T(8,128)(2,1)}), bf16[128,1024]{1,0:T(8,128)(2,1)}) %reduce-scatter.7.cloned.1.call-update) | async-done | bytes 262160
  731.0 16.4 all_to_all.20
  747.7 4.5 multiply_bitcast_fusion
  752.2 9.0 copy.242
  761.3 3.4 fusion.83
  764.7 3.7 fusion.85
  772.1 1303.9 %reduce-scatter.9.cloned.1.call-done = f32[16,512]{1,0:T(8,128)} async-done(((f32[4096,512]{1,0:T(8,128)}), f32[16,512]{1,0:T(8,128)}) %reduce-scatter.9.cloned.1.call-update) | async-done | bytes 32784
  (132 shorter events, 65.7 us)
Async XLA Ops:
  7.2 417.8 %copy-start = (bf16[1,128,4096]{2,1,0:T(8,128)(2,1)S(1)}, bf16[1,128,4096]{2,1,0:T(8,128)(2,1)}, u32[]{:S(2)}) copy-start(bf16[1,128,4096]{2,1,0:T(8,128)(2,1)} %param.9) | copy-start | bytes 3145732
  7.2 439.6 %copy-start.21 = (bf16[1,128,4096]{2,1,0:T(8,128)(2,1)S(1)}, bf16[1,128,4096]{2,1,0:T(8,128)(2,1)}, u32[]{:S(2)}) copy-start(bf16[1,128,4096]{2,1,0:T(8,128)(2,1)} %param.14) | copy-start | bytes 3145732
  7.2 417.8 %all-gather.3.cloned.1.call-start = ((), (), s32[]{:S(2)}) async-start(), calls=%async_computation.6 | async-start | bytes 4210688 | tf_op jit(solution)/shard_map/all_gather | solution.py:53
  429.9 15.9 all-to-all-start
  433.4 55.7 %copy-start.28 = (s32[1,8]{1,0:T(1,128)S(1)}, s32[1,8]{1,0:T(1,128)}, u32[]{:S(2)}) copy-start(s32[1,8]{1,0:T(1,128)} %param.15) | copy-start | bytes 100
  433.5 56.1 %copy-start.27 = (s32[1,32,32]{2,1,0:T(8,128)S(1)}, s32[1,32,32]{2,1,0:T(8,128)}, u32[]{:S(2)}) copy-start(s32[1,32,32]{2,1,0:T(8,128)} %param.17) | copy-start | bytes 12292
  433.5 108.5 %all-gather.5.cloned.1.call-start = ((), (), s32[]{:S(2)}) async-start(), calls=%async_computation.7 | async-start | bytes 4456448 | tf_op jit(solution)/shard_map/all_gather | solution.py:97
  448.8 35.8 %all-to-all-start.2 = ((bf16[16,16,4096]{2,1,0:T(8,128)(2,1)}), bf16[16,16,4096]{2,1,0:T(8,128)(2,1)S(1)}, u32[]{:S(2)}, u32[]{:S(2)}) async-start(bf16[16,16,4096]{2,1,0:T(8,128)(2,1)} %bitcast.340), calls=%async_computation.2 | async-start | bytes 4194304 | tf_op jit(solution)/shard_map/all_to_all | solution.py:91
  484.6 6.9 copy-start.8
  484.6 44.9 %all-to-all-start.1 = ((bf16[16,16,4096]{2,1,0:T(8,128)(2,1)}), bf16[16,16,4096]{2,1,0:T(8,128)(2,1)}, u32[]{:S(2)}, u32[]{:S(2)}) async-start(bf16[16,16,4096]{2,1,0:T(8,128)(2,1)} %bitcast.338), calls=%async_computation.1 | async-start | bytes 4194304 | tf_op jit(solution)/shard_map/all_to_all | solution.py:90
  489.1 240.6 %reduce-scatter.7.cloned.1.call-start = ((), (), s32[]{:S(2)}) async-start(), calls=%async_computation.8 | async-start | bytes 4456448
  494.5 85.1 %copy-start.10 = (pred[128,2048]{0,1:T(8,128)(4,1)}, pred[128,2048]{0,1:T(8,128)(4,1)S(1)}, u32[]{:S(2)}) copy-start(pred[128,2048]{0,1:T(8,128)(4,1)S(1)} %copy.165) | copy-start | bytes 786436
  541.9 36.3 %copy-start.18 = (bf16[128,1,8,128]{3,2,1,0:T(8,128)(2,1)}, bf16[128,1,8,128]{3,2,1,0:T(8,128)(2,1)S(1)}, u32[]{:S(2)}) copy-start(bf16[128,1,8,128]{3,2,1,0:T(8,128)(2,1)S(1)} %get-tuple-element.51) | copy-start | bytes 786436
  554.6 8.9 copy-start.2
  563.5 5.6 copy-start.16
  563.5 14.8 copy-start.14
  567.9 4.6 copy-start.26
  585.4 4.5 copy-start.1
  597.2 6.7 copy-start.20
  597.2 9.1 copy-start.11
  603.9 8.6 copy-start.4
  606.3 6.2 copy-start.19
  606.3 10.7 copy-start.22
  617.0 6.3 copy-start.17
  623.3 6.1 slice-start
  623.3 6.1 copy-start.25
  625.6 3.8 slice-start.1
  643.8 1432.2 %reduce-scatter.9.cloned.1.call-start = ((), (), s32[]{:S(2)}) async-start(), calls=%async_computation.9 | async-start | bytes 8421376
  761.2 7.2 copy-start.13
  761.2 7.2 copy-start.5
  761.3 7.9 copy-start.7
  761.3 7.9 copy-start.12
  (6 other events, 16.4 us)
Sparse Core Ops, SparseCore 0:
  9.9 414.9 all-gather.2
  446.9 80.7 all-gather.4
  644.0 85.6 reduce-scatter.6
  761.4 1314.6 reduce-scatter.8
where the time goes:
time: 2090 us; the launch traced here: 2080 us
  waiting for transfers between devices  1870 us (89%)
  matrix products  81.8 us (4%)
  local copies, waits for them, and re-layouts  67.4 us (3%)
  other arithmetic  24.6 us (1%)
    unnamed x6, waiting for transfers between devices  1390 us
    all_gather x1, waiting for transfers between devices, local(): lax.all_gather(value_weight, ('dp', 'ctx'), axis=0, tiled=True)  406 us
  transfers between devices with their start and end apart: 7, of which 6 were waited for; matrix products, arithmetic and copies ran while one was open for 2% of the time, Pallas kernels for 0%

commit v1 on v0

--- a/solution.py
+++ b/solution.py
@@ -9,6 +9,11 @@
 HD = 128
 VB = 64
 far_below = -1e30
+
+
+def all_by_exchange(block, name, along):
+    sent = jnp.stack([block] * lax.axis_size(name))
+    return jnp.concatenate(lax.all_to_all(sent, name, 0, 0), axis=along)
 
 
 def document_index(positions, doc_lengths):
@@ -49,9 +54,7 @@
     block_count = block_table.shape[0]
     columns = features
     projected = jnp.dot(
-        columns,
-        lax.all_gather(value_weight, ("dp", "ctx"), axis=0, tiled=True),
-        preferred_element_type=jnp.float32,
+        columns, all_by_exchange(value_weight, ("dp", "ctx"), 0), preferred_element_type=jnp.float32
     )
     value_rows = projected.astype(jnp.bfloat16)
     token_iota = jnp.arange(token_count, dtype=jnp.int32)

time: 2090 us -> 1790 us (0.86)
  waiting for transfers between devices: 1870 us -> 1540 us
    all_gather x1 -> x0, waiting for transfers between devices: 406 us -> none  [local(): lax.all_gather(value_weight, ('dp', 'ctx'), axis=0, tiled=True)]
    all_to_all x0 -> x1, waiting for transfers between devices: none -> 83.2 us  [all_by_exchange(): return jnp.concatenate(lax.all_to_all(sent, name, 0, 0), axis=along)]
    unnamed x6 -> x5, waiting for transfers between devices: 1390 us -> 1390 us
  transfers between devices with their start and end apart: 7 -> 7, of which waited for: 6 -> 6; matrix products, arithmetic and copies ran while one was open for 2% -> 3% of each run, Pallas kernels for 0% -> 0%
where the time goes in v1:
time: 1790 us; the launch traced here: 1780 us
  waiting for transfers between devices  1540 us (86%)
  matrix products  81.2 us (5%)
  local copies, waits for them, and re-layouts  70.8 us (4%)
  starting transfers between devices  27.5 us (2%)
  other arithmetic  21 us (1%)
    unnamed x5, waiting for transfers between devices  1390 us
    all_to_all x1, waiting for transfers between devices, all_by_exchange(): return jnp.concatenate(lax.all_to_all(sent, name, 0, 0), axis=along)  83.2 us
  transfers between devices with their start and end apart: 7, of which 6 were waited for; matrix products, arithmetic and copies ran while one was open for 3% of the time, Pallas kernels for 0%

profile of v1, /device:TPU:128, one launch (start us, length us, event | category | flops | bytes accessed | tf_op | source)
XLA Modules:
  0.0 1776.2 jit_solution(10640993222210446982)
XLA Ops:
  10.5 14.8 all-to-all-start
  25.4 8.0 scatter_custom_fusion
  34.0 83.2 %all-to-all-done = bf16[256,16,512]{2,1,0:T(8,128)(2,1)} async-done(((bf16[256,16,512]{2,1,0:T(8,128)(2,1)}), bf16[256,16,512]{2,1,0:T(8,128)(2,1)}, u32[]{:S(2)}, u32[]{:S(2)}) %all-to-all-start) | async-done | bytes 4194336 | tf_op jit(solution)/shard_map/all_to_all | solution.py:16
  121.2 4.4 all-to-all-start.1
  127.3 10.8 all-to-all-done.1
  141.1 3.7 all-to-all-start.3
  148.0 28.8 %all-to-all-done.3 = bf16[16,16,4096]{2,1,0:T(8,128)(2,1)S(1)} async-done(((bf16[16,16,4096]{2,1,0:T(8,128)(2,1)}), bf16[16,16,4096]{2,1,0:T(8,128)(2,1)S(1)}, u32[]{:S(2)}, u32[]{:S(2)}) %all-to-all-start.3) | async-done | bytes 2097184 | tf_op jit(solution)/shard_map/all_to_all | solution.py:94
  176.9 4.4 all-to-all-start.2
  190.8 31.0 %all-to-all-done.2 = bf16[16,16,4096]{2,1,0:T(8,128)(2,1)} async-done(((bf16[16,16,4096]{2,1,0:T(8,128)(2,1)}), bf16[16,16,4096]{2,1,0:T(8,128)(2,1)}, u32[]{:S(2)}, u32[]{:S(2)}) %all-to-all-start.2) | async-done | bytes 2097184 | tf_op jit(solution)/shard_map/all_to_all | solution.py:93
  234.2 4.6 fusion.140
  238.7 4.2 reshape.219
  242.9 4.0 reshape.213
  246.9 8.9 fusion.142
  255.8 4.3 fusion.141
  261.4 3.4 fusion.17
  264.8 3.6 fusion.16
  272.0 3.4 fusion.7
  277.9 4.5 fusion.12
  284.9 4.5 fusion.2
  289.4 6.7 fusion.11
  298.5 6.2 fusion.6
  304.8 4.5 fusion.53
  309.3 4.4 fusion.1
  317.9 3.8 fusion.68
  329.7 6.4 copy.240
  336.2 86.7 %reduce-scatter.7.cloned.1.call-done = bf16[128,1024]{1,0:T(8,128)(2,1)} async-done(((bf16[2048,1024]{1,0:T(8,128)(2,1)}), bf16[128,1024]{1,0:T(8,128)(2,1)}) %reduce-scatter.7.cloned.1.call-update) | async-done | bytes 262160
  424.2 16.5 all_to_all.25
  441.0 4.5 multiply_bitcast_fusion
  445.4 9.0 copy.242
  454.5 3.4 fusion.83
  457.9 3.7 fusion.85
  465.3 1303.9 %reduce-scatter.9.cloned.1.call-done = f32[16,512]{1,0:T(8,128)} async-done(((f32[4096,512]{1,0:T(8,128)}), f32[16,512]{1,0:T(8,128)}) %reduce-scatter.9.cloned.1.call-update) | async-done | bytes 32784
  (136 shorter events, 67.4 us)
Async XLA Ops:
  7.2 110.0 %copy-start = (bf16[1,128,4096]{2,1,0:T(8,128)(2,1)S(1)}, bf16[1,128,4096]{2,1,0:T(8,128)(2,1)}, u32[]{:S(2)}) copy-start(bf16[1,128,4096]{2,1,0:T(8,128)(2,1)} %param.9) | copy-start | bytes 3145732
  7.2 18.2 %copy-start.28 = (s32[1,2048]{1,0:T(1,128)S(1)}, s32[1,2048]{1,0:T(1,128)}, u32[]{:S(2)}) copy-start(s32[1,2048]{1,0:T(1,128)} %param.16) | copy-start | bytes 24580
  7.2 112.9 %copy-start.27 = (bf16[1,128,512]{2,1,0:T(8,128)(2,1)S(1)}, bf16[1,128,512]{2,1,0:T(8,128)(2,1)}, u32[]{:S(2)}) copy-start(bf16[1,128,512]{2,1,0:T(8,128)(2,1)} %param.12) | copy-start | bytes 393220
  10.5 128.5 %copy-start.21 = (bf16[1,128,4096]{2,1,0:T(8,128)(2,1)S(1)}, bf16[1,128,4096]{2,1,0:T(8,128)(2,1)}, u32[]{:S(2)}) copy-start(bf16[1,128,4096]{2,1,0:T(8,128)(2,1)} %param.14) | copy-start | bytes 3145732
  10.5 106.7 %all-to-all-start = ((bf16[256,16,512]{2,1,0:T(8,128)(2,1)}), bf16[256,16,512]{2,1,0:T(8,128)(2,1)}, u32[]{:S(2)}, u32[]{:S(2)}) async-start(bf16[256,16,512]{2,1,0:T(8,128)(2,1)} %stack.17), calls=%async_computation | async-start | bytes 8388608 | tf_op jit(solution)/shard_map/all_to_all | solution.py:16
  121.2 16.8 all-to-all-start.1
  125.6 55.7 %copy-start.30 = (s32[1,8]{1,0:T(1,128)S(1)}, s32[1,8]{1,0:T(1,128)}, u32[]{:S(2)}) copy-start(s32[1,8]{1,0:T(1,128)} %param.15) | copy-start | bytes 100
  125.7 56.1 %copy-start.29 = (s32[1,32,32]{2,1,0:T(8,128)S(1)}, s32[1,32,32]{2,1,0:T(8,128)}, u32[]{:S(2)}) copy-start(s32[1,32,32]{2,1,0:T(8,128)} %param.17) | copy-start | bytes 12292
  125.7 108.5 %all-gather.2.cloned.1.call-start = ((), (), s32[]{:S(2)}) async-start(), calls=%async_computation.7 | async-start | bytes 4456448 | tf_op jit(solution)/shard_map/all_gather | solution.py:100
  141.1 35.8 %all-to-all-start.3 = ((bf16[16,16,4096]{2,1,0:T(8,128)(2,1)}), bf16[16,16,4096]{2,1,0:T(8,128)(2,1)S(1)}, u32[]{:S(2)}, u32[]{:S(2)}) async-start(bf16[16,16,4096]{2,1,0:T(8,128)(2,1)} %bitcast.341), calls=%async_computation.3 | async-start | bytes 4194304 | tf_op jit(solution)/shard_map/all_to_all | solution.py:94
  176.9 6.9 copy-start.8
  176.9 44.9 %all-to-all-start.2 = ((bf16[16,16,4096]{2,1,0:T(8,128)(2,1)}), bf16[16,16,4096]{2,1,0:T(8,128)(2,1)}, u32[]{:S(2)}, u32[]{:S(2)}) async-start(bf16[16,16,4096]{2,1,0:T(8,128)(2,1)} %bitcast.339), calls=%async_computation.2 | async-start | bytes 4194304 | tf_op jit(solution)/shard_map/all_to_all | solution.py:93
  181.3 241.6 %reduce-scatter.7.cloned.1.call-start = ((), (), s32[]{:S(2)}) async-start(), calls=%async_computation.8 | async-start | bytes 4456448
  186.8 85.2 %copy-start.10 = (pred[128,2048]{0,1:T(8,128)(4,1)}, pred[128,2048]{0,1:T(8,128)(4,1)S(1)}, u32[]{:S(2)}) copy-start(pred[128,2048]{0,1:T(8,128)(4,1)S(1)} %copy.165) | copy-start | bytes 786436
  234.2 36.6 %copy-start.18 = (bf16[128,1,8,128]{3,2,1,0:T(8,128)(2,1)}, bf16[128,1,8,128]{3,2,1,0:T(8,128)(2,1)S(1)}, u32[]{:S(2)}) copy-start(bf16[128,1,8,128]{3,2,1,0:T(8,128)(2,1)S(1)} %get-tuple-element.51) | copy-start | bytes 786436
  246.9 8.9 copy-start.2
  255.8 5.6 copy-start.16
  255.8 15.0 copy-start.14
  260.1 4.6 copy-start.26
  289.4 6.7 copy-start.20
  289.4 9.1 copy-start.11
  296.2 8.6 copy-start.4
  298.5 6.2 copy-start.19
  298.5 10.7 copy-start.22
  309.3 6.3 copy-start.17
  315.6 6.1 slice-start
  315.6 6.1 copy-start.25
  336.1 1433.1 %reduce-scatter.9.cloned.1.call-start = ((), (), s32[]{:S(2)}) async-start(), calls=%async_computation.9 | async-start | bytes 8421376
  454.4 7.2 copy-start.13
  454.5 7.2 copy-start.5
  454.5 8.0 copy-start.7
  454.5 8.0 copy-start.12
  (8 other events, 24.7 us)
Sparse Core Ops, SparseCore 0:
  139.1 81.7 all-gather.1
  336.3 86.5 reduce-scatter.6
  454.6 1314.5 reduce-scatter.8
